TPU v7x, 32 devices: a whole 2x2x4 slice. The times are simulated.
32 devices in a mesh: groups: 2 (over y), chan: 4 (over z), win: 4 (over x, core).
Axes of the slice: x: 2, y: 2, z: 4, core: 2. Of those that a mesh axis runs over, the one named last changes fastest.
Arguments:
- tokens: bfloat16 [8, 1024, 512], P(('groups', 'win'), 'chan'), parts along dimension 0, may hold values from -6 to 6
- head_weight: bfloat16 [512, 1024], replicated, may hold values from -0.25 to 0.25
- target: bfloat16 [8, 512, 2048], P(('groups', 'win'), 'chan'), parts along dimension 0, may hold values from -6 to 6
- target_amp: bfloat16 [8, 512, 2048], P(('groups', 'win'), 'chan'), parts along dimension 0, may hold values from 0.29882812 to 3
- patch_ranks: int32 [8, 1024], P(('groups', 'win'), 'chan'), parts along dimension 0, may hold values from 0 to 1023, each once within a row
Outputs:
- grad_tokens: bfloat16 [8, 1024, 512], P(('groups', 'win'), 'chan'), parts along dimension 0
- grad_weight: float32 [1024, 1024], P(('groups', 'chan'), 'win'), parts along dimension 0
There are 2 independent parts, one for each index of `groups`. A program takes and returns all parts, laid end to end along the dimension named above; an argument that names none is the same for every part. Nothing has to cross between parts.
Inputs may be any that keep to these rules, and one draw needn't show every extreme that they name: `patch_ranks`: each window's row is a permutation of 0 to 1023; a patch is masked exactly when its rank is 256 or more.
All inputs are finite; a program needn't handle non-finite values.
Results may differ from a plain program's by a relative error of at most 0.0052.
Values sent between devices are 32-bit elements; how exact they have to be, the bound alone decides.
A program may use at most 128 MiB of HBM per device.

v0:
```python
from functools import partial
import math
import jax
import jax.numpy as jnp
from jax import lax
from jax.sharding import PartitionSpec as P

PATCH_C = 16
PATCH_S = 64
product = partial(jnp.einsum, precision=lax.Precision.HIGHEST)


def factor_pair(length):
    first = int(math.isqrt(length))
    while length % first:
        first -= 1
    return (first, length // first)


def section_one(length, direction):
    index = jnp.arange(length, dtype=jnp.int32)
    angles = (
        direction
        * 2.0
        * math.pi
        / length
        * (index[:, None] * index[None, :] % length).astype(jnp.float32)
    )
    cosine = jnp.cos(angles)
    sine = jnp.sin(angles)
    upper = jnp.stack([cosine, sine], axis=1)
    lower = jnp.stack([-sine, cosine], axis=1)
    return jnp.stack([upper, lower], axis=0)


def section_two(first, second, direction, scale):
    length = first * second
    outer = jnp.arange(first, dtype=jnp.int32)[:, None, None]
    inner = jnp.arange(second, dtype=jnp.int32)[None, :, None]
    final = jnp.arange(second, dtype=jnp.int32)[None, None, :]
    phase = (outer * inner + first * inner * final) % length
    angles = direction * 2.0 * math.pi / length * phase.astype(jnp.float32)
    cosine = jnp.cos(angles)
    sine = jnp.sin(angles)
    upper = jnp.stack([cosine, sine], axis=2)
    lower = jnp.stack([-sine, cosine], axis=2)
    return jnp.stack([upper, lower], axis=0) * scale


def time_forward(values):
    window_count, chan_rows, length = values.shape
    first, second = factor_pair(length)
    shaped = values.reshape(window_count, chan_rows, first, second)
    section = product("wcab,ask->wsckb", shaped, section_one(first, -1.0)[0])
    result = product("wsckb,skbtj->wtcjk", section, section_two(first, second, -1.0, 1.0))
    return result.reshape(window_count, 2, chan_rows, length)


def time_inverse(spectrum, scale):
    window_count, _, chan_rows, length = spectrum.shape
    first, second = factor_pair(length)
    shaped = spectrum.reshape(window_count, 2, chan_rows, first, second)
    section = product("wrcab,rask->wsckb", shaped, section_one(first, 1.0))
    result = product(
        "wsckb,skbj->wcjk", section, section_two(first, second, 1.0, scale)[:, :, :, 0, :]
    )
    return result.reshape(window_count, chan_rows, length)


def channel_transform(spectrum, direction, scale):
    window_count, _, length, columns = spectrum.shape
    first, second = factor_pair(length)
    shaped = spectrum.reshape(window_count, 2, first, second, columns)
    section = product("wrabm,rask->wskbm", shaped, section_one(first, direction))
    result = product("wskbm,skbtj->wtjkm", section, section_two(first, second, direction, scale))
    return result.reshape(window_count, 2, length, columns)


def per_device(tokens, head_weight, target, target_amp, patch_ranks):
    chan_count = lax.axis_size("chan")
    win_count = lax.axis_size("win")
    local_windows, local_patches, width = tokens.shape
    local_channels = target.shape[1]
    samples = target.shape[2]
    all_channels = local_channels * chan_count
    all_windows = local_windows * win_count
    channel_patches = local_channels // PATCH_C
    sample_patches = samples // PATCH_S
    pixels = PATCH_C * PATCH_S
    keep_count = local_patches * chan_count // 4
    column_count = samples // chan_count
    norm_scale = 1.0 / math.sqrt(all_channels * samples)
    patches = jnp.einsum(
        "wpe,ef->wpf", tokens, head_weight, preferred_element_type=jnp.float32
    ).astype(jnp.bfloat16)
    image = patches.reshape(local_windows, channel_patches, sample_patches, PATCH_C, PATCH_S)
    image = image.transpose(0, 1, 3, 2, 4).reshape(local_windows, local_channels, samples)
    masked = (patch_ranks >= keep_count).reshape(
        local_windows, channel_patches, 1, sample_patches, 1
    )
    pixel_mask = jnp.broadcast_to(
        masked, (local_windows, channel_patches, PATCH_C, sample_patches, PATCH_S)
    )
    pixel_mask = pixel_mask.reshape(local_windows, local_channels, samples)
    composite = jnp.where(pixel_mask, image, target)
    time_spectrum = time_forward(composite.astype(jnp.float32))
    amp_full = target_amp.astype(jnp.float32)
    spectrum = time_spectrum.reshape(local_windows, 2, local_channels, chan_count, column_count)
    amp_blocks = amp_full.reshape(local_windows, 1, local_channels, chan_count, column_count)
    spectrum_cols, amp_cols = (
        lax.all_to_all(spectrum, "chan", split_axis=3, concat_axis=2, tiled=True),
        lax.all_to_all(amp_blocks, "chan", split_axis=3, concat_axis=2, tiled=True),
    )
    freq = channel_transform(spectrum_cols[:, :, :, 0, :], -1.0, norm_scale)
    freq_real = freq[:, 0]
    freq_imag = freq[:, 1]
    amplitude = jnp.sqrt(freq_real * freq_real + freq_imag * freq_imag + 1.0)
    weighting = (amplitude - amp_cols[:, 0, :, 0, :]) / (amplitude * all_windows)
    back = channel_transform(freq * weighting[:, None], 1.0, 1.0)
    residual_cols = back[:, :, :, None, :]
    returned = lax.all_to_all(residual_cols, "chan", split_axis=2, concat_axis=3, tiled=True)
    returned = returned.reshape(local_windows, 2, local_channels, samples)
    image_real = time_inverse(returned, norm_scale)
    grad_image = jnp.where(pixel_mask, image_real, 0.0)
    grad_patches = grad_image.reshape(
        local_windows, channel_patches, PATCH_C, sample_patches, PATCH_S
    )
    grad_patches = (
        grad_patches.transpose(0, 1, 3, 2, 4)
        .reshape(local_windows, local_patches, pixels)
        .astype(jnp.bfloat16)
    )
    grad_tokens = jnp.einsum(
        "wpf,ef->wpe", grad_patches, head_weight, preferred_element_type=jnp.float32
    ).astype(jnp.bfloat16)
    own_rows = lax.psum_scatter(
        jnp.einsum("wpe,wpf->ef", tokens, grad_patches, preferred_element_type=jnp.float32),
        "chan",
        scatter_dimension=0,
        tiled=True,
    )
    grad_weight = lax.psum_scatter(own_rows, "win", scatter_dimension=1, tiled=True)
    return (grad_tokens, grad_weight)


def solution(mesh):
    in_specs = (
        P(("groups", "win"), "chan", None),
        P(),
        P(("groups", "win"), "chan", None),
        P(("groups", "win"), "chan", None),
        P(("groups", "win"), "chan"),
    )
    out_specs = (P(("groups", "win"), "chan", None), P(("groups", "chan"), "win"))
    return jax.shard_map(
        per_device, mesh=mesh, in_specs=in_specs, out_specs=out_specs, check_vma=False
    )
```

profile of v0, /device:TPU:0, one launch (start us, length us, event | category | flops | bytes accessed | tf_op | source)
XLA Modules:
  0.0 274.6 jit_solution(7919645180658135055)
XLA Ops:
  7.2 1.4 copy.107
  9.7 6.3 %all-to-all-start.1 = ((f32[1,1,128,4,512]{2,4,1,0,3:T(8,128)}), f32[1,1,128,4,512]{2,4,1,0,3:T(8,128)S(1)}, u32[]{:S(2)}, u32[]{:S(2)}) async-start(f32[1,1,128,4,512]{2,4,1,0,3:T(8,128)} %convert.2), calls=%async_computation.1 | async-start | bytes 2097152 | tf_op jit(solution)/shard_map/all_to_all | solution.py:112
  18.5 1.8 reshape.543
  20.2 1.3 copy.191
  21.5 2.0 reshape.544
  26.2 9.3 %multiply_sine_fusion.1 = (f32[32,64,1,64]{1,3,2,0:T(8,128)}, f32[32,64,1,64]{1,3,2,0:T(8,128)S(1)}, f32[32,64,1,64]{1,3,2,0:T(8,128)}, f32[32,64,1,64]{1,3,2,0:...) fusion(s32[64,64]{0,1:T(8,128)S(1)} %iota_multiply_fusion, s32[32,64]{1,0:T(8,128)S(1)} %iota_multiply_fusion.2), kind=kLoop, calls=%fused_computation.67 | loop fusion | flops 2228224 | bytes 3170304 | tf_op jit(solution)/shard_map/sin | solution.py:44
  36.1 5.1 %fusion.36 = f32[1,2,128,64,32]{2,3,1,4,0:T(8,128)S(1)} fusion(f32[2,128,32,64,1]{1,2,3,0,4:T(8,128)S(1)} %convolution_bitcast_fusion.1, f32[1,32,64,2,64]{2,4,0,3,1:T(8,128)S(1)} %get-tuple-element.15, f32[1,32,64,2,64]{2,4,0,3,1:T(8,128)S(1)} %get-tuple-element.14), kind=kOutput, calls=%fused_computation.37 | convolution fusion | flops 805830656 | bytes 6291456 | tf_op jit(solution)/shard_map/wsckb,skbtj->wtcjk/dot_general | solution.py:55
  42.5 1.5 copy.101
  44.9 5.1 %all-to-all-start = ((f32[1,2,128,4,512]{2,4,1,0,3:T(8,128)}), f32[1,2,128,4,512]{2,4,1,0,3:T(8,128)S(1)}, u32[]{:S(2)}, u32[]{:S(2)}) async-start(f32[1,2,128,4,512]{2,4,1,0,3:T(8,128)} %copy.101), calls=%async_computation | async-start | bytes 4194304 | tf_op jit(solution)/shard_map/all_to_all | solution.py:111
  50.3 2.0 multiply_sine_fusion.3
  54.5 2.6 copy.109
  57.1 40.5 %all-to-all-done = f32[1,2,128,4,512]{2,4,1,0,3:T(8,128)S(1)} async-done(((f32[1,2,128,4,512]{2,4,1,0,3:T(8,128)}), f32[1,2,128,4,512]{2,4,1,0,3:T(8,128)S(1)}, u32[]{:S(2)}, u32[]{:S(2)}) %all-to-all-start) | async-done | bytes 2097184 | tf_op jit(solution)/shard_map/all_to_all | solution.py:111
  97.6 2.0 copy.102
  99.6 4.6 %fusion.24 = f32[2,16,32,512,1]{3,1,2,0,4:T(8,128)S(1)} fusion(f32[2,16,32,512]{3,2,1,0:T(8,128)} %bitcast.180, f32[1,16,2,16]{1,3,0,2:T(8,128)S(1)} %get-tuple-element.37, f32[1,16,2,16]{1,3,0,2:T(8,128)S(1)} %get-tuple-element.36), kind=kOutput, calls=%fused_computation.33 | convolution fusion | flops 201327616 | bytes 4198400 | tf_op jit(solution)/shard_map/wrabm,rask->wskbm/dot_general | solution.py:74
  104.3 3.0 %fusion.27 = f32[1,2,32,16,512]{4,2,1,3,0:T(8,128)S(1)} fusion(f32[2,16,32,512,1]{3,1,2,0,4:T(8,128)S(1)} %fusion.24, f32[1,16,32,2,32]{2,4,0,3,1:T(8,128)S(1)} %copy-done.7, f32[1,16,32,2,32]{2,4,0,3,1:T(8,128)S(1)} %copy-done.6), kind=kOutput, calls=%fused_computation.34 | convolution fusion | flops 402784256 | bytes 4456448 | tf_op jit(solution)/shard_map/wskbm,skbtj->wtjkm/dot_general | solution.py:75
  109.6 3.0 %fusion.30 = f32[2,16,32,512,1]{3,1,2,0,4:T(8,128)S(1)} fusion(f32[2,16,32,512]{3,2,1,0:T(8,128)S(1)} %broadcast_multiply_fusion, f32[1,16,2,16]{1,3,2,0:T(8,128)S(1)} %get-tuple-element.35, f32[1,16,2,16]{1,3,2,0:T(8,128)S(1)} %get-tuple-element.34), kind=kOutput, calls=%fused_computation.35 | convolution fusion | flops 201327616 | bytes 4198400 | tf_op jit(solution)/shard_map/wrabm,rask->wskbm/dot_general | solution.py:74
  112.6 3.3 %fusion.11 = f32[16,2,32,512,1]{3,2,1,0,4:T(8,128)S(1)} fusion(f32[2,16,32,512,1]{3,1,2,0,4:T(8,128)S(1)} %fusion.30, f32[1,16,32,2,32]{2,4,3,1,0:T(8,128)S(1)} %copy-done.5, f32[1,16,32,2,32]{2,4,3,1,0:T(8,128)S(1)} %copy-done.4), kind=kOutput, calls=%fused_computation.15 | convolution fusion | flops 402718720 | bytes 4456448 | tf_op jit(solution)/shard_map/wskbm,skbtj->wtjkm/dot_general | solution.py:75
  117.4 3.0 %copy.115 = f32[1,2,512,1,512]{4,1,3,0,2:T(2,128)} copy(f32[1,2,512,1,512]{4,2,1,3,0:T(8,128)S(1)} %bitcast.184) | data formatting | bytes 4194304 | tf_op jit(solution)/shard_map/broadcast_in_dim;reshape | solution.py:120
  120.4 4.5 %all-to-all-start.2 = ((f32[1,2,512,1,512]{4,1,3,0,2:T(2,128)}), f32[1,2,512,1,512]{4,1,3,0,2:T(2,128)}, u32[]{:S(2)}, u32[]{:S(2)}) async-start(f32[1,2,512,1,512]{4,1,3,0,2:T(2,128)} %copy.115), calls=%async_computation.2 | async-start | bytes 4194304 | tf_op jit(solution)/shard_map/all_to_all | solution.py:121
  125.1 4.3 %maximum_bitcast_fusion = (f32[1,32,64,2,64]{2,4,3,1,0:T(8,128)S(1)}, f32[1,32,64,2,64]{2,4,3,1,0:T(8,128)}) fusion(f32[32,64,1,64]{1,3,2,0:T(8,128)} %get-tuple-element.20, f32[32,64,1,64]{1,3,2,0:T(8,128)} %get-tuple-element.25, f32[32,64,1,64]{1,3,2,0:T(8,128)} %get-tuple-element.22), kind=kLoop, calls=%fused_computation.9 | loop fusion | flops 524288 | bytes 3670016 | tf_op jit(solution)/shard_map/stack | solution.py:47
  129.4 43.2 %all-to-all-done.2 = f32[1,2,512,1,512]{4,1,3,0,2:T(2,128)} async-done(((f32[1,2,512,1,512]{4,1,3,0,2:T(2,128)}), f32[1,2,512,1,512]{4,1,3,0,2:T(2,128)}, u32[]{:S(2)}, u32[]{:S(2)}) %all-to-all-start.2) | async-done | bytes 2097184 | tf_op jit(solution)/shard_map/all_to_all | solution.py:121
  172.6 3.4 %copy.116 = f32[1,2,512,1,512]{4,2,1,3,0:T(8,128)} copy(f32[1,2,512,1,512]{4,1,3,0,2:T(2,128)} %all-to-all-done.2) | data formatting | bytes 4194304 | tf_op jit(solution)/shard_map/all_to_all | solution.py:121
  175.9 3.1 %copy.117 = f32[1,2,128,4,1,512]{2,5,3,1,4,0:T(8,128)} copy(f32[1,2,128,4,1,512]{5,2,3,1,4,0:T(8,128)} %bitcast.185) | data formatting | bytes 4194304 | tf_op jit(solution)/shard_map/all_to_all | solution.py:121
  179.0 4.7 %fusion.33 = f32[2,128,32,64]{1,2,3,0:T(8,128)S(1)} fusion(f32[2,128,32,64]{1,3,2,0:T(8,128)} %bitcast.181, f32[1,32,2,32]{1,3,2,0:T(8,128)S(1)} %get-tuple-element.33, f32[1,32,2,32]{1,3,2,0:T(8,128)S(1)} %get-tuple-element.32), kind=kOutput, calls=%fused_computation.36 | convolution fusion | flops 402657280 | bytes 4210688 | tf_op jit(solution)/shard_map/wrcab,rask->wsckb/dot_general | solution.py:63
  183.8 4.3 %fusion.41 = bf16[1,128,64,32]{1,2,3,0:T(8,128)(2,1)} fusion(f32[2,128,32,64]{1,2,3,0:T(8,128)S(1)} %fusion.33, f32[1,32,64,2,64]{2,4,3,1,0:T(8,128)S(1)} %copy-done.1, f32[1,32,64,2,64]{2,4,3,1,0:T(8,128)S(1)} %get-tuple-element.12), kind=kOutput, calls=%fused_computation.42 | convolution fusion | flops 403177472 | bytes 4718592 | tf_op jit(solution)/shard_map/wsckb,skbj->wcjk/dot_general | solution.py:64
  188.1 4.5 %copy.121 = bf16[1,128,64,32]{3,2,1,0:T(8,128)(2,1)S(1)} copy(bf16[1,128,64,32]{1,2,3,0:T(8,128)(2,1)} %fusion.41) | data formatting | bytes 1048576 | tf_op jit(solution)/shard_map/wsckb,skbj->wcjk/transpose | solution.py:64
  192.6 1.8 reshape.554
  194.4 1.5 fusion.49
  197.1 1.8 convolution_bitcast_fusion
  198.9 43.1 %reduce-scatter.3.cloned.1.call-done = f32[128,1024]{0,1:T(8,128)} async-done(((f32[512,1024]{0,1:T(8,128)}), f32[128,1024]{0,1:T(8,128)}) %reduce-scatter.3.cloned.1.call-update) | async-done | bytes 524304 | tf_op jit(solution)/shard_map/reduce_scatter | solution.py:136
  243.2 22.4 %reduce-scatter.5.cloned.1.call-done = f32[128,256]{0,1:T(8,128)} async-done(((f32[128,1024]{0,1:T(8,128)}), f32[128,256]{0,1:T(8,128)}) %reduce-scatter.5.cloned.1.call-update) | async-done | bytes 131088 | tf_op jit(solution)/shard_map/reduce_scatter | solution.py:142
  265.7 1.7 copy.123
  (64 shorter events, 17.8 us)
Async XLA Ops:
  7.2 8.9 %copy-start = (bf16[512,1024]{1,0:T(8,128)(2,1)S(1)}, bf16[512,1024]{1,0:T(8,128)(2,1)}, u32[]{:S(2)}) copy-start(bf16[512,1024]{1,0:T(8,128)(2,1)} %param.6) | copy-start | bytes 3145732
  8.6 7.4 %copy-start.10 = (s32[1,256]{1,0:T(1,128)S(1)}, s32[1,256]{1,0:T(1,128)}, u32[]{:S(2)}) copy-start(s32[1,256]{1,0:T(1,128)} %param.9) | copy-start | bytes 3076
  8.6 7.4 %copy-start.8 = (bf16[1,256,512]{2,1,0:T(8,128)(2,1)S(1)}, bf16[1,256,512]{2,1,0:T(8,128)(2,1)}, u32[]{:S(2)}) copy-start(bf16[1,256,512]{2,1,0:T(8,128)(2,1)} %param.5) | copy-start | bytes 786436
  9.7 34.3 %all-to-all-start.1 = ((f32[1,1,128,4,512]{2,4,1,0,3:T(8,128)}), f32[1,1,128,4,512]{2,4,1,0,3:T(8,128)S(1)}, u32[]{:S(2)}, u32[]{:S(2)}) async-start(f32[1,1,128,4,512]{2,4,1,0,3:T(8,128)} %convert.2), calls=%async_computation.1 | async-start | bytes 2097152 | tf_op jit(solution)/shard_map/all_to_all | solution.py:112
  43.9 1.0 copy-start.2
  44.9 52.7 %all-to-all-start = ((f32[1,2,128,4,512]{2,4,1,0,3:T(8,128)}), f32[1,2,128,4,512]{2,4,1,0,3:T(8,128)S(1)}, u32[]{:S(2)}, u32[]{:S(2)}) async-start(f32[1,2,128,4,512]{2,4,1,0,3:T(8,128)} %copy.101), calls=%async_computation | async-start | bytes 4194304 | tf_op jit(solution)/shard_map/all_to_all | solution.py:111
  99.6 4.6 %copy-start.6 = (f32[1,16,32,2,32]{2,4,0,3,1:T(8,128)S(1)}, f32[1,16,32,2,32]{2,4,0,3,1:T(8,128)}, u32[]{:S(2)}) copy-start(f32[1,16,32,2,32]{2,4,0,3,1:T(8,128)} %get-tuple-element.18) | copy-start | bytes 393220
  99.6 4.6 %copy-start.7 = (f32[1,16,32,2,32]{2,4,0,3,1:T(8,128)S(1)}, f32[1,16,32,2,32]{2,4,0,3,1:T(8,128)}, u32[]{:S(2)}) copy-start(f32[1,16,32,2,32]{2,4,0,3,1:T(8,128)} %get-tuple-element.19) | copy-start | bytes 393220
  107.3 1.2 copy-start.3
  109.6 3.0 %copy-start.4 = (f32[1,16,32,2,32]{2,4,3,1,0:T(8,128)S(1)}, f32[1,16,32,2,32]{2,4,3,1,0:T(8,128)}, u32[]{:S(2)}) copy-start(f32[1,16,32,2,32]{2,4,3,1,0:T(8,128)} %get-tuple-element.16) | copy-start | bytes 393220
  109.6 3.0 %copy-start.5 = (f32[1,16,32,2,32]{2,4,3,1,0:T(8,128)S(1)}, f32[1,16,32,2,32]{2,4,3,1,0:T(8,128)}, u32[]{:S(2)}) copy-start(f32[1,16,32,2,32]{2,4,3,1,0:T(8,128)} %get-tuple-element.17) | copy-start | bytes 393220
  120.4 52.2 %all-to-all-start.2 = ((f32[1,2,512,1,512]{4,1,3,0,2:T(2,128)}), f32[1,2,512,1,512]{4,1,3,0,2:T(2,128)}, u32[]{:S(2)}, u32[]{:S(2)}) async-start(f32[1,2,512,1,512]{4,1,3,0,2:T(2,128)} %copy.115), calls=%async_computation.2 | async-start | bytes 4194304 | tf_op jit(solution)/shard_map/all_to_all | solution.py:121
  124.8 117.2 %reduce-scatter.3.cloned.1.call-start = ((), (), s32[]{:S(2)}) async-start(), calls=%async_computation.5 | async-start | bytes 2621440 | tf_op jit(solution)/shard_map/reduce_scatter | solution.py:136
  179.0 4.8 %copy-start.1 = (f32[1,32,64,2,64]{2,4,3,1,0:T(8,128)S(1)}, f32[1,32,64,2,64]{2,4,3,1,0:T(8,128)}, u32[]{:S(2)}) copy-start(f32[1,32,64,2,64]{2,4,3,1,0:T(8,128)} %get-tuple-element.13) | copy-start | bytes 3145732
  195.9 1.2 copy-start.9
  198.9 66.8 %reduce-scatter.5.cloned.1.call-start = ((), (), s32[]{:S(2)}) async-start(), calls=%async_computation.6 | async-start | bytes 655360 | tf_op jit(solution)/shard_map/reduce_scatter | solution.py:142
Sparse Core Ops, SparseCore 0:
  199.0 42.9 reduce-scatter.2
  244.7 20.9 reduce-scatter.4
where the time goes:
time: 280 us; the launch traced here: 275 us
  waiting for transfers between devices  149 us (53%)
  local copies, waits for them, and re-layouts  37.3 us (13%)
  matrix products  33.3 us (12%)
  other arithmetic  23.8 us (8%)
  starting transfers between devices  15.9 us (6%)
  between operations  14.9 us (5%)
    all_to_all x1, waiting for transfers between devices, per_device(): lax.all_to_all(residual_cols, 'chan', split_axis=2, concat_axis=3, tiled=...  43.2 us
    reduce_scatter x1, waiting for transfers between devices, per_device(): lax.psum_scatter(jnp.einsum('wpe,wpf->ef', tokens, grad_patches, preferre...  43.1 us
    all_to_all x1, waiting for transfers between devices, per_device(): lax.all_to_all(spectrum, 'chan', split_axis=3, concat_axis=2, tiled=True)  40.5 us
    reduce_scatter x1, waiting for transfers between devices, per_device(): lax.psum_scatter(own_rows, 'win', scatter_dimension=1, tiled=True)  22.4 us
    sin x2, other arithmetic, section_two(): sine = jnp.sin(angles)  11.2 us
    dot_general x2, matrix products, channel_transform(): product('wrabm,rask->wskbm', shaped, section_one(first, direction))  7.62 us
    another operation x4, other arithmetic, section_two(): return jnp.stack([upper, lower], axis=0) * scale  7.17 us
    all_to_all x2, local copies, waits for them, and re-layouts, per_device(): lax.all_to_all(residual_cols, 'chan', split_axis=2, concat_axis=3, tiled=...  6.44 us
  transfers between devices with their start and end apart: 5, of which 4 were waited for; matrix products, arithmetic and copies ran while one was open for 15% of the time, Pallas kernels for 0%

commit v1 on v0

--- a/solution.py
+++ b/solution.py
@@ -8,6 +8,22 @@
 PATCH_C = 16
 PATCH_S = 64
 product = partial(jnp.einsum, precision=lax.Precision.HIGHEST)
+
+
+def pairwise_exchange(array, axis, split, join):
+    ways, here = (lax.axis_size(axis), lax.axis_index(axis))
+    width = array.shape[split] // ways
+    shape = list(array.shape)
+    shape[split] = width
+    height = shape[join]
+    shape[join] = height * ways
+    full = jnp.zeros(shape, array.dtype)
+    for mask in range(ways):
+        part = lax.dynamic_slice_in_dim(array, (here ^ mask) * width, width, axis=split)
+        if mask:
+            part = lax.ppermute(part, axis, [(d, d ^ mask) for d in range(ways)])
+        full = lax.dynamic_update_slice_in_dim(full, part, (here ^ mask) * height, axis=join)
+    return full
 
 
 def factor_pair(length):
@@ -109,7 +125,7 @@
     amp_blocks = amp_full.reshape(local_windows, 1, local_channels, chan_count, column_count)
     spectrum_cols, amp_cols = (
         lax.all_to_all(spectrum, "chan", split_axis=3, concat_axis=2, tiled=True),
-        lax.all_to_all(amp_blocks, "chan", split_axis=3, concat_axis=2, tiled=True),
+        pairwise_exchange(amp_blocks, "chan", 3, 2),
     )
     freq = channel_transform(spectrum_cols[:, :, :, 0, :], -1.0, norm_scale)
     freq_real = freq[:, 0]

time: 280 us -> 293 us (1.046)
  local copies, waits for them, and re-layouts: 37.3 us -> 46.1 us
  other arithmetic: 23.8 us -> 26.9 us
  waiting for transfers between devices: 149 us -> 152 us
    ppermute x0 -> x3, waiting for transfers between devices: none -> 41.3 us  [pairwise_exchange(): part = lax.ppermute(part, axis, [(d, d ^ mask) for d in range(ways)])]
    all_to_all x1, waiting for transfers between devices: 40.5 us -> 0.01 us  [per_device(): lax.all_to_all(spectrum, 'chan', split_axis=3, concat_axis=2, tiled=True)]
    all_to_all x1 -> x0, starting transfers between devices: 6.32 us -> none  [per_device(): lax.all_to_all(amp_blocks, 'chan', split_axis=3, concat_axis=2, tiled=True)]
    dynamic_update_slice x0 -> x4, local copies, waits for them, and re-layouts: none -> 5.73 us  [pairwise_exchange(): lax.dynamic_update_slice_in_dim(full, part, (here ^ mask) * height, axis=...]
    unnamed x24 -> x21, local copies, waits for them, and re-layouts: 4.07 us -> 9.11 us
    ppermute x0 -> x3, starting transfers between devices: none -> 4.39 us  [pairwise_exchange(): part = lax.ppermute(part, axis, [(d, d ^ mask) for d in range(ways)])]
  transfers between devices with their start and end apart: 5 -> 7, of which waited for: 4 -> 5; matrix products, arithmetic and copies ran while one was open for 15% -> 10% of each run, Pallas kernels for 0% -> 0%
where the time goes in v1:
time: 293 us; the launch traced here: 288 us
  waiting for transfers between devices  152 us (52%)
  local copies, waits for them, and re-layouts  46.1 us (16%)
  matrix products  33.4 us (11%)
  other arithmetic  26.9 us (9%)
  starting transfers between devices  15.7 us (5%)
  between operations  14.9 us (5%)
    reduce_scatter x1, waiting for transfers between devices, per_device(): lax.psum_scatter(jnp.einsum('wpe,wpf->ef', tokens, grad_patches, preferre...  44.4 us
    all_to_all x1, waiting for transfers between devices, per_device(): lax.all_to_all(residual_cols, 'chan', split_axis=2, concat_axis=3, tiled=...  43.4 us
    ppermute x3, waiting for transfers between devices, pairwise_exchange(): part = lax.ppermute(part, axis, [(d, d ^ mask) for d in range(ways)])  41.3 us
    reduce_scatter x1, waiting for transfers between devices, per_device(): lax.psum_scatter(own_rows, 'win', scatter_dimension=1, tiled=True)  22.4 us
    sin x2, other arithmetic, section_two(): sine = jnp.sin(angles)  11.3 us
    unnamed x21, local copies, waits for them, and re-layouts  9.11 us
    dot_general x2, matrix products, channel_transform(): product('wrabm,rask->wskbm', shaped, section_one(first, direction))  7.62 us
    another operation x4, other arithmetic, section_two(): return jnp.stack([upper, lower], axis=0) * scale  7.16 us
  transfers between devices with their start and end apart: 7, of which 5 were waited for; matrix products, arithmetic and copies ran while one was open for 10% of the time, Pallas kernels for 0%

profile of v1, /device:TPU:0, one launch (start us, length us, event | category | flops | bytes accessed | tf_op | source)
XLA Modules:
  0.0 288.5 jit_solution(6791045913425150805)
XLA Ops:
  13.9 9.4 %multiply_sine_fusion.1 = (f32[32,64,1,64]{1,3,2,0:T(8,128)}, f32[32,64,1,64]{1,3,2,0:T(8,128)S(1)}, f32[32,64,1,64]{1,3,2,0:T(8,128)}, f32[32,64,1,64]{1,3,2,0:...) fusion(s32[64,64]{0,1:T(8,128)S(1)} %iota_multiply_fusion, s32[32,64]{1,0:T(8,128)S(1)} %iota_multiply_fusion.2), kind=kLoop, calls=%fused_computation.67 | loop fusion | flops 2228224 | bytes 3170304 | tf_op jit(solution)/shard_map/sin | solution.py:60
  24.9 5.1 %fusion.36 = f32[1,2,128,64,32]{2,3,1,4,0:T(8,128)S(1)} fusion(f32[2,128,32,64,1]{1,2,3,0,4:T(8,128)S(1)} %convolution_bitcast_fusion.1, f32[1,32,64,2,64]{2,4,0,3,1:T(8,128)S(1)} %get-tuple-element.19, f32[1,32,64,2,64]{2,4,0,3,1:T(8,128)S(1)} %get-tuple-element.18), kind=kOutput, calls=%fused_computation.37 | convolution fusion | flops 805830656 | bytes 6291456 | tf_op jit(solution)/shard_map/wsckb,skbtj->wtcjk/dot_general | solution.py:71
  32.7 6.5 %all-to-all-start = ((f32[1,2,128,4,512]{2,4,1,0,3:T(8,128)}), f32[1,2,128,4,512]{2,4,1,0,3:T(8,128)S(1)}, u32[]{:S(2)}, u32[]{:S(2)}) async-start(f32[1,2,128,4,512]{2,4,1,0,3:T(8,128)} %copy.106), calls=%async_computation | async-start | bytes 4194304 | tf_op jit(solution)/shard_map/all_to_all | solution.py:127
  39.2 2.0 copy.112
  41.3 2.1 convert.1
  43.4 2.1 constant_dynamic-slice_fusion
  45.5 1.8 copy.155
  47.2 2.0 collective-permute-start
  49.3 1.8 copy.156
  51.0 2.4 collective-permute-start.1
  53.4 1.8 copy.157
  56.3 2.0 multiply_sine_fusion.3
  62.4 17.6 %collective-permute-done = f32[1,1,128,1,512]{4,2,3,1,0:T(8,128)} collective-permute-done((f32[1,1,128,1,512]{4,2,3,1,0:T(8,128)}, f32[1,1,128,1,512]{4,2,3,1,0:T(8,128)}, u32[]{:S(2)}, u32[]{:S(2)}) %collective-permute-start) | collective-permute-done | bytes 262176 | tf_op jit(solution)/shard_map/ppermute | solution.py:24
  81.6 23.8 %collective-permute-done.1 = f32[1,1,128,1,512]{4,2,3,1,0:T(8,128)} collective-permute-done((f32[1,1,128,1,512]{4,2,3,1,0:T(8,128)}, f32[1,1,128,1,512]{4,2,3,1,0:T(8,128)}, u32[]{:S(2)}, u32[]{:S(2)}) %collective-permute-start.1) | collective-permute-done | bytes 262176 | tf_op jit(solution)/shard_map/ppermute | solution.py:24
  108.7 1.8 copy.107
  110.6 4.6 %fusion.24 = f32[2,16,32,512,1]{3,1,2,0,4:T(8,128)S(1)} fusion(f32[2,16,32,512]{3,2,1,0:T(8,128)} %bitcast.181, f32[1,16,2,16]{1,3,0,2:T(8,128)S(1)} %get-tuple-element.41, f32[1,16,2,16]{1,3,0,2:T(8,128)S(1)} %get-tuple-element.40), kind=kOutput, calls=%fused_computation.33 | convolution fusion | flops 201327616 | bytes 4198400 | tf_op jit(solution)/shard_map/wrabm,rask->wskbm/dot_general | solution.py:90
  115.2 3.0 %fusion.27 = f32[1,2,32,16,512]{4,2,1,3,0:T(8,128)S(1)} fusion(f32[2,16,32,512,1]{3,1,2,0,4:T(8,128)S(1)} %fusion.24, f32[1,16,32,2,32]{2,4,0,3,1:T(8,128)S(1)} %copy-done.5, f32[1,16,32,2,32]{2,4,0,3,1:T(8,128)S(1)} %copy-done.4), kind=kOutput, calls=%fused_computation.34 | convolution fusion | flops 402784256 | bytes 4456448 | tf_op jit(solution)/shard_map/wskbm,skbtj->wtjkm/dot_general | solution.py:91
  121.7 3.0 %fusion.30 = f32[2,16,32,512,1]{3,1,2,0,4:T(8,128)S(1)} fusion(f32[2,16,32,512]{3,2,1,0:T(8,128)S(1)} %broadcast_multiply_fusion, f32[1,16,2,16]{1,3,2,0:T(8,128)S(1)} %get-tuple-element.39, f32[1,16,2,16]{1,3,2,0:T(8,128)S(1)} %get-tuple-element.38), kind=kOutput, calls=%fused_computation.35 | convolution fusion | flops 201327616 | bytes 4198400 | tf_op jit(solution)/shard_map/wrabm,rask->wskbm/dot_general | solution.py:90
  124.8 3.3 %fusion.11 = f32[16,2,32,512,1]{3,2,1,0,4:T(8,128)S(1)} fusion(f32[2,16,32,512,1]{3,1,2,0,4:T(8,128)S(1)} %fusion.30, f32[1,16,32,2,32]{2,4,3,1,0:T(8,128)S(1)} %copy-done.3, f32[1,16,32,2,32]{2,4,3,1,0:T(8,128)S(1)} %copy-done.2), kind=kOutput, calls=%fused_computation.15 | convolution fusion | flops 402718720 | bytes 4456448 | tf_op jit(solution)/shard_map/wskbm,skbtj->wtjkm/dot_general | solution.py:91
  129.6 3.0 %copy.122 = f32[1,2,512,1,512]{4,1,3,0,2:T(2,128)} copy(f32[1,2,512,1,512]{4,2,1,3,0:T(8,128)S(1)} %bitcast.185) | data formatting | bytes 4194304 | tf_op jit(solution)/shard_map/broadcast_in_dim;reshape | solution.py:136
  132.5 4.7 %all-to-all-start.1 = ((f32[1,2,512,1,512]{4,1,3,0,2:T(2,128)}), f32[1,2,512,1,512]{4,1,3,0,2:T(2,128)}, u32[]{:S(2)}, u32[]{:S(2)}) async-start(f32[1,2,512,1,512]{4,1,3,0,2:T(2,128)} %copy.122), calls=%async_computation.1 | async-start | bytes 4194304 | tf_op jit(solution)/shard_map/all_to_all | solution.py:137
  137.5 4.3 %maximum_bitcast_fusion = (f32[1,32,64,2,64]{2,4,3,1,0:T(8,128)S(1)}, f32[1,32,64,2,64]{2,4,3,1,0:T(8,128)}) fusion(f32[32,64,1,64]{1,3,2,0:T(8,128)} %get-tuple-element.24, f32[32,64,1,64]{1,3,2,0:T(8,128)} %get-tuple-element.29, f32[32,64,1,64]{1,3,2,0:T(8,128)} %get-tuple-element.26), kind=kLoop, calls=%fused_computation.9 | loop fusion | flops 524288 | bytes 3670016 | tf_op jit(solution)/shard_map/stack | solution.py:63
  141.8 43.4 %all-to-all-done.1 = f32[1,2,512,1,512]{4,1,3,0,2:T(2,128)} async-done(((f32[1,2,512,1,512]{4,1,3,0,2:T(2,128)}), f32[1,2,512,1,512]{4,1,3,0,2:T(2,128)}, u32[]{:S(2)}, u32[]{:S(2)}) %all-to-all-start.1) | async-done | bytes 2097184 | tf_op jit(solution)/shard_map/all_to_all | solution.py:137
  185.2 3.4 %copy.123 = f32[1,2,512,1,512]{4,2,1,3,0:T(8,128)} copy(f32[1,2,512,1,512]{4,1,3,0,2:T(2,128)} %all-to-all-done.1) | data formatting | bytes 4194304 | tf_op jit(solution)/shard_map/all_to_all | solution.py:137
  188.5 3.1 %copy.124 = f32[1,2,128,4,1,512]{2,5,3,1,4,0:T(8,128)} copy(f32[1,2,128,4,1,512]{5,2,3,1,4,0:T(8,128)} %bitcast.186) | data formatting | bytes 4194304 | tf_op jit(solution)/shard_map/all_to_all | solution.py:137
  191.6 4.7 %fusion.33 = f32[2,128,32,64]{1,2,3,0:T(8,128)S(1)} fusion(f32[2,128,32,64]{1,3,2,0:T(8,128)} %bitcast.182, f32[1,32,2,32]{1,3,2,0:T(8,128)S(1)} %get-tuple-element.37, f32[1,32,2,32]{1,3,2,0:T(8,128)S(1)} %get-tuple-element.36), kind=kOutput, calls=%fused_computation.36 | convolution fusion | flops 402657280 | bytes 4210688 | tf_op jit(solution)/shard_map/wrcab,rask->wsckb/dot_general | solution.py:79
  196.4 4.3 %fusion.41 = bf16[1,128,64,32]{1,2,3,0:T(8,128)(2,1)} fusion(f32[2,128,32,64]{1,2,3,0:T(8,128)S(1)} %fusion.33, f32[1,32,64,2,64]{2,4,3,1,0:T(8,128)S(1)} %copy-done.1, f32[1,32,64,2,64]{2,4,3,1,0:T(8,128)S(1)} %get-tuple-element.12), kind=kOutput, calls=%fused_computation.42 | convolution fusion | flops 403177472 | bytes 4718592 | tf_op jit(solution)/shard_map/wsckb,skbj->wcjk/dot_general | solution.py:80
  200.6 4.5 %copy.128 = bf16[1,128,64,32]{3,2,1,0:T(8,128)(2,1)S(1)} copy(bf16[1,128,64,32]{1,2,3,0:T(8,128)(2,1)} %fusion.41) | data formatting | bytes 1048576 | tf_op jit(solution)/shard_map/wsckb,skbj->wcjk/transpose | solution.py:80
  205.2 1.8 reshape.601
  209.6 1.8 convolution_bitcast_fusion
  211.5 44.4 %reduce-scatter.3.cloned.1.call-done = f32[128,1024]{0,1:T(8,128)} async-done(((f32[512,1024]{0,1:T(8,128)}), f32[128,1024]{0,1:T(8,128)}) %reduce-scatter.3.cloned.1.call-update) | async-done | bytes 524304 | tf_op jit(solution)/shard_map/reduce_scatter | solution.py:152
  257.1 22.4 %reduce-scatter.5.cloned.1.call-done = f32[128,256]{0,1:T(8,128)} async-done(((f32[128,1024]{0,1:T(8,128)}), f32[128,256]{0,1:T(8,128)}) %reduce-scatter.5.cloned.1.call-update) | async-done | bytes 131088 | tf_op jit(solution)/shard_map/reduce_scatter | solution.py:158
  (71 shorter events, 31.9 us)
Async XLA Ops:
  7.2 2.1 copy-start
  32.7 76.0 %all-to-all-start = ((f32[1,2,128,4,512]{2,4,1,0,3:T(8,128)}), f32[1,2,128,4,512]{2,4,1,0,3:T(8,128)S(1)}, u32[]{:S(2)}, u32[]{:S(2)}) async-start(f32[1,2,128,4,512]{2,4,1,0,3:T(8,128)} %copy.106), calls=%async_computation | async-start | bytes 4194304 | tf_op jit(solution)/shard_map/all_to_all | solution.py:127
  47.2 32.7 %collective-permute-start = (f32[1,1,128,1,512]{4,2,3,1,0:T(8,128)}, f32[1,1,128,1,512]{4,2,3,1,0:T(8,128)}, u32[]{:S(2)}, u32[]{:S(2)}) collective-permute-start(f32[1,1,128,1,512]{4,2,3,1,0:T(8,128)} %copy.155), channel_id=1, source_target_pairs={{0,4},{4,0},{8,12},{12,8},{1,5},{5,1},{9,13},{13,9},{2,6},{6,2},{1... | collective-permute-start | bytes 786440 | tf_op jit(solution)/shard_map/ppermute | solution.py:24
  51.0 54.4 %collective-permute-start.1 = (f32[1,1,128,1,512]{4,2,3,1,0:T(8,128)}, f32[1,1,128,1,512]{4,2,3,1,0:T(8,128)}, u32[]{:S(2)}, u32[]{:S(2)}) collective-permute-start(f32[1,1,128,1,512]{4,2,3,1,0:T(8,128)} %copy.156), channel_id=1, source_target_pairs={{0,8},{4,12},{8,0},{12,4},{1,9},{5,13},{9,1},{13,5},{2,10},{6,14},... | collective-permute-start | bytes 786440 | tf_op jit(solution)/shard_map/ppermute | solution.py:24
  55.2 51.9 %collective-permute-start.2 = (f32[1,1,128,1,512]{4,2,3,1,0:T(8,128)}, f32[1,1,128,1,512]{4,2,3,1,0:T(8,128)}, u32[]{:S(2)}, u32[]{:S(2)}) collective-permute-start(f32[1,1,128,1,512]{4,2,3,1,0:T(8,128)} %copy.157), channel_id=1, source_target_pairs={{0,12},{4,8},{8,4},{12,0},{1,13},{5,9},{9,5},{13,1},{2,14},{6,10},... | collective-permute-start | bytes 786440 | tf_op jit(solution)/shard_map/ppermute | solution.py:24
  56.3 4.2 %copy-start.6 = (f32[1,1,128,1,512]{4,2,3,1,0:T(8,128)S(1)}, f32[1,1,128,1,512]{4,2,3,1,0:T(8,128)}, u32[]{:S(2)}) copy-start(f32[1,1,128,1,512]{4,2,3,1,0:T(8,128)} %copy.113) | copy-start | bytes 786436
  110.6 4.6 %copy-start.4 = (f32[1,16,32,2,32]{2,4,0,3,1:T(8,128)S(1)}, f32[1,16,32,2,32]{2,4,0,3,1:T(8,128)}, u32[]{:S(2)}) copy-start(f32[1,16,32,2,32]{2,4,0,3,1:T(8,128)} %get-tuple-element.22) | copy-start | bytes 393220
  110.6 4.6 %copy-start.5 = (f32[1,16,32,2,32]{2,4,0,3,1:T(8,128)S(1)}, f32[1,16,32,2,32]{2,4,0,3,1:T(8,128)}, u32[]{:S(2)}) copy-start(f32[1,16,32,2,32]{2,4,0,3,1:T(8,128)} %get-tuple-element.23) | copy-start | bytes 393220
  121.7 3.0 %copy-start.2 = (f32[1,16,32,2,32]{2,4,3,1,0:T(8,128)S(1)}, f32[1,16,32,2,32]{2,4,3,1,0:T(8,128)}, u32[]{:S(2)}) copy-start(f32[1,16,32,2,32]{2,4,3,1,0:T(8,128)} %get-tuple-element.20) | copy-start | bytes 393220
  121.7 3.0 %copy-start.3 = (f32[1,16,32,2,32]{2,4,3,1,0:T(8,128)S(1)}, f32[1,16,32,2,32]{2,4,3,1,0:T(8,128)}, u32[]{:S(2)}) copy-start(f32[1,16,32,2,32]{2,4,3,1,0:T(8,128)} %get-tuple-element.21) | copy-start | bytes 393220
  132.5 52.6 %all-to-all-start.1 = ((f32[1,2,512,1,512]{4,1,3,0,2:T(2,128)}), f32[1,2,512,1,512]{4,1,3,0,2:T(2,128)}, u32[]{:S(2)}, u32[]{:S(2)}) async-start(f32[1,2,512,1,512]{4,1,3,0,2:T(2,128)} %copy.122), calls=%async_computation.1 | async-start | bytes 4194304 | tf_op jit(solution)/shard_map/all_to_all | solution.py:137
  137.3 118.6 %reduce-scatter.3.cloned.1.call-start = ((), (), s32[]{:S(2)}) async-start(), calls=%async_computation.4 | async-start | bytes 2621440 | tf_op jit(solution)/shard_map/reduce_scatter | solution.py:152
  191.6 4.7 %copy-start.1 = (f32[1,32,64,2,64]{2,4,3,1,0:T(8,128)S(1)}, f32[1,32,64,2,64]{2,4,3,1,0:T(8,128)}, u32[]{:S(2)}) copy-start(f32[1,32,64,2,64]{2,4,3,1,0:T(8,128)} %get-tuple-element.13) | copy-start | bytes 3145732
  208.5 1.2 copy-start.7
  211.4 68.1 %reduce-scatter.5.cloned.1.call-start = ((), (), s32[]{:S(2)}) async-start(), calls=%async_computation.5 | async-start | bytes 655360 | tf_op jit(solution)/shard_map/reduce_scatter | solution.py:158
Sparse Core Ops, SparseCore 0:
  211.6 44.2 reduce-scatter.2
  258.5 20.9 reduce-scatter.4
